TPU v7x, 32 devices: a whole 2x2x4 slice. The times are simulated.
32 devices in a mesh: cfg: 1, pair: 16 (over z, y, x), blk: 2 (over core).
Axes of the slice: x: 2, y: 2, z: 4, core: 2. Of those that a mesh axis runs over, the one named last changes fastest.
Arguments:
- elementals: bfloat16 [16, 8, 2, 65536], P('cfg', None, None, ('pair', 'blk')), may hold values from -0.079589844 to 0.079589844
- perambulator: bfloat16 [16, 2, 1024, 1024], P(('cfg', 'pair'), None, None, 'blk'), may hold values from -0.1875 to 0.1875
- pairs: int32 [16, 2], replicated, may hold values from 0 to 15, as said below
- elem_index: int32 [16, 24], replicated, may hold values from 0 to 7
- coef_code: int32 [16, 24, 4, 4], replicated, may hold values from -2 to 2
- term_count: int32 [16], replicated, may hold values from 12 to 24, as said below
Outputs:
- correlator: float32 [16, 2], P(('cfg', 'pair'))
Inputs may be any that keep to these rules, and one draw needn't show every extreme that they name: `pairs`: pair p + 8 lists the two timeslices of pair p in reverse order; the two timeslices of a pair differ. `term_count`: some pair uses all 24 terms.
All inputs are finite; a program needn't handle non-finite values.
Results may differ from a plain program's by a relative error of at most 0.0057.
Values may be sent and summed in bfloat16 or wider, within the bound.
A program may use at most 64 MiB of HBM per device.

v0:
```python
import jax
import jax.numpy as jnp
from jax import lax
from jax.sharding import PartitionSpec as P

NV = 256
NS = 4


def partner(value, axis, apart):
    return lax.ppermute(value, axis, [(i, i ^ 1 << apart) for i in range(lax.axis_size(axis))])


def shards(elementals, perambulator, pairs, elem_index, coef_code, term_count):
    peers = lax.axis_size("pair")
    entries = elementals.shape[-1]
    nterms = elem_index.shape[1]
    used = (jnp.arange(nterms)[None, :] < term_count[:, None]).astype(jnp.float32)
    weights = (coef_code.astype(jnp.float32) * 0.5 * used[:, :, None, None]).astype(jnp.bfloat16)
    picked = elementals[pairs[:, 0][:, None], elem_index]
    combined = jnp.einsum(
        "pkab,pkcf->pabcf", weights, picked, preferred_element_type=jnp.float32
    ).astype(jnp.bfloat16)
    blocks = lax.all_to_all(combined, "pair", split_axis=0, concat_axis=0, tiled=True)
    gathered = lax.all_gather(blocks[:, None], "blk", axis=1, tiled=True)
    propagator = perambulator[0]
    columns = propagator.shape[-1]
    shaped = gathered.reshape(2 * peers, NS, NS, 2, entries // NV, NV)
    phi_real = shaped[:, :, :, 0]
    phi_imag = shaped[:, :, :, 1]
    prop_real = propagator[0].reshape(NS, NV, columns)
    prop_imag = propagator[1].reshape(NS, NV, columns)
    form = "gabuj,bjn->agun"
    dressed_real = jnp.einsum(
        form, phi_real, prop_real, preferred_element_type=jnp.float32
    ) - jnp.einsum(form, phi_imag, prop_imag, preferred_element_type=jnp.float32)
    dressed_imag = jnp.einsum(
        form, phi_real, prop_imag, preferred_element_type=jnp.float32
    ) + jnp.einsum(form, phi_imag, prop_real, preferred_element_type=jnp.float32)
    dressed = (
        jnp.stack([dressed_real, dressed_imag]).astype(jnp.bfloat16).reshape(2, NS * NV, columns)
    )
    mirror_bit = peers.bit_length() - 2
    mirror = partner(dressed, "pair", mirror_bit)
    mirror_rows = lax.all_to_all(mirror, "blk", split_axis=1, concat_axis=2, tiled=True)
    products = jnp.einsum("zrc,ycr->zy", dressed, mirror_rows, preferred_element_type=jnp.float32)
    partial_trace = jnp.stack([products[0, 0] - products[1, 1], products[0, 1] + products[1, 0]])
    total = lax.psum(partial_trace, "blk")
    return total[None, :]


def solution(mesh):
    return jax.shard_map(
        shards,
        mesh=mesh,
        in_specs=(
            P("cfg", None, None, ("pair", "blk")),
            P(("cfg", "pair"), None, None, "blk"),
            P(),
            P(),
            P(),
            P(),
        ),
        out_specs=P(("cfg", "pair"), None),
        check_vma=False,
    )
```

profile of v0, /device:TPU:0, one launch (start us, length us, event | category | flops | bytes accessed | tf_op | source)
XLA Modules:
  0.0 274.8 jit_solution(7903193112295483595)
XLA Ops:
  6.5 0.0 copy-start
  6.5 0.0 all-gather.3.cloned.1.call-start
  6.5 0.8 fusion.23
  7.3 0.8 fusion.19
  8.1 0.1 reshape.44
  8.2 0.7 fusion.20
  8.9 0.0 copy-done
  8.9 0.0 copy-start.6
  8.9 19.1 %gather_fusion = bf16[384,2,2048]{2,1,0:T(2,128)(2,1)} fusion(bf16[16,8,2,2048]{3,2,1,0:T(2,128)(2,1)S(1)} %copy-done, s32[384]{0:T(512)S(1)} %reshape.44), kind=kCustom, calls=%fused_computation | custom fusion | bytes 6294528 | tf_op jit(solution)/shard_map/gather | solution.py:20
  28.0 0.0 copy-done.6
  28.0 4.5 %fusion.2 = bf16[16,4,4,2,2048]{4,2,3,1,0:T(4,128)(2,1)S(1)} fusion(bf16[16,24,2,2048,1]{3,2,1,0,4:T(2,128)(2,1)} %bitcast.96, s32[16,24,4,4]{1,3,2,0:T(4,128)S(1)} %copy-done.6, f32[16,24]{1,0:T(8,128)S(1)} %fusion.20), kind=kOutput, calls=%fused_computation.3 | convolution fusion | flops 51398656 | bytes 5268992 | tf_op jit(solution)/shard_map/pkab,pkcf->pabcf/dot_general | solution.py:21
  32.5 57.1 %all_to_all.23 = bf16[16,4,4,2,2048]{4,2,3,1,0:T(4,128)(2,1)} all-to-all(bf16[16,4,4,2,2048]{4,2,3,1,0:T(4,128)(2,1)S(1)} %fusion.2), channel_id=1, replica_groups=mesh['cfg'=1,'pair'=16,'blk'=2] {'pair'}, dimensions={0} | all-to-all | bytes 4194304 | tf_op jit(solution)/shard_map/all_to_all | solution.py:24
  89.6 0.0 copy-start.3
  89.6 0.0 all-gather.3.cloned.1.call-update
  89.6 1.6 copy-done.3
  91.1 1.5 fusion.24
  92.6 0.0 copy-start.4
  92.6 9.0 %all-gather.3.cloned.1.call-done = bf16[16,8,4,2,2048]{4,2,3,1,0:T(4,128)(2,1)} async-done(((bf16[16,4,4,2,2048]{4,2,3,1,0:T(4,128)(2,1)}), bf16[16,8,4,2,2048]{4,2,3,1,0:T(4,128)(2,1)}) %all-gather.3.cloned.1.call-update) | async-done | bytes 4194320 | tf_op jit(solution)/shard_map/all_gather | solution.py:25
  101.7 7.7 %reshape.43 = bf16[32,4,4,2,8,256]{5,4,2,3,1,0:T(8,128)(2,1)} reshape(bf16[16,8,4,2,2048]{4,2,3,1,0:T(4,128)(2,1)} %all-gather.3.cloned.1.call-done) | data formatting | bytes 8388608 | tf_op jit(solution)/shard_map/reshape | solution.py:28
  109.4 0.0 copy-done.4
  109.4 0.0 copy-start.1
  109.4 0.0 copy-start.5
  109.4 3.0 %fusion.7 = f32[32,4,8,512,1]{3,2,4,1,0:T(8,128)S(1)} fusion(bf16[4,256,512,1,1]{2,1,0,4,3:T(8,128)(2,1)S(1)} %bitcast.102, bf16[32,4,4,2,8,256]{5,4,2,3,1,0:T(8,128)(2,1)} %reshape.43), kind=kOutput, calls=%fused_computation.12 | convolution fusion | flops 1073741824 | bytes 5242880 | tf_op jit(solution)/shard_map/gabuj,bjn->agun/dot_general | solution.py:37
  112.4 0.0 copy-done.1
  112.4 0.1 copy-done.5
  112.5 2.6 fusion.8
  115.1 1.2 fusion.12
  116.3 1.1 copy.32
  117.4 4.7 %copy.34 = bf16[1,1024,512]{1,0,2:T(2,128)(2,1)S(1)} copy(bf16[1,1024,512]{2,1,0:T(8,128)(2,1)} %bitcast.99) | data formatting | bytes 2097152 | tf_op jit(solution)/shard_map/stack | solution.py:41
  122.2 3.8 %fusion.11 = bf16[4,32,8,512]{3,2,0,1:T(8,128)(2,1)S(1)} fusion(bf16[4,256,512,1,1]{2,1,0,4,3:T(8,128)(2,1)} %bitcast.101, bf16[32,4,4,2,8,256]{5,4,2,3,1,0:T(8,128)(2,1)} %reshape.43, f32[32,4,8,512,1]{3,2,4,1,0:T(8,128)} %fusion.8), kind=kOutput, calls=%fused_computation.16 | convolution fusion | flops 1074790400 | bytes 6291456 | tf_op jit(solution)/shard_map/gabuj,bjn->agun/dot_general | solution.py:36
  126.0 1.1 copy.31
  127.0 6.0 %copy.33 = bf16[1,1024,512]{1,0,2:T(2,128)(2,1)} copy(bf16[1,1024,512]{2,1,0:T(8,128)(2,1)} %bitcast.100) | data formatting | bytes 2097152 | tf_op jit(solution)/shard_map/stack | solution.py:41
  133.0 5.9 %pad_maximum_fusion = bf16[2,1024,512]{1,0,2:T(2,128)(2,1)S(1)} fusion(bf16[1,1024,512]{1,0,2:T(2,128)(2,1)S(1)} %copy.34, bf16[1,1024,512]{1,0,2:T(2,128)(2,1)} %copy.33), kind=kLoop, calls=%fused_computation.6 | loop fusion | flops 4194304 | bytes 4194304 | tf_op jit(solution)/shard_map/stack | solution.py:41
  138.9 0.0 copy-start.2
  138.9 2.7 collective-permute-start
  141.6 0.0 copy-done.2
  141.6 91.1 %collective-permute-done = bf16[2,1024,512]{1,0,2:T(2,128)(2,1)} collective-permute-done((bf16[2,1024,512]{1,0,2:T(2,128)(2,1)S(1)}, bf16[2,1024,512]{1,0,2:T(2,128)(2,1)}, u32[]{:S(2)}, u32[]{:S(2)}) %collective-permute-start) | collective-permute-done | bytes 2097184 | tf_op jit(solution)/shard_map/ppermute | solution.py:11
  232.8 8.3 %copy.35 = bf16[2,1024,512]{2,0,1:T(2,128)(2,1)S(1)} copy(bf16[2,1024,512]{1,0,2:T(2,128)(2,1)} %collective-permute-done) | data formatting | bytes 4194304 | tf_op jit(solution)/shard_map/ppermute | solution.py:11
  241.1 5.4 %all_to_all.24 = bf16[2,1024,512]{2,0,1:T(2,128)(2,1)S(1)} all-to-all(bf16[2,1024,512]{2,0,1:T(2,128)(2,1)S(1)} %copy.35), channel_id=1, replica_groups=mesh['cfg'=1,'pair'=16,'blk'=2] {'blk'}, dimensions={1} | all-to-all | bytes 4194304 | tf_op jit(solution)/shard_map/all_to_all | solution.py:45
  246.5 3.2 %copy.54 = bf16[2,2,512,512]{3,1,0,2:T(2,128)(2,1)S(1)} copy(bf16[2,2,512,512]{3,0,2,1:T(2,128)(2,1)S(1)} %bitcast.97) | data formatting | bytes 4194304 | tf_op jit(solution)/shard_map/all_to_all | solution.py:45
  249.8 2.6 all_to_all.20
  252.4 9.3 %convolution_bitcast_fusion = f32[2,2]{1,0:T(2,128)S(1)} fusion(bf16[2,1024,512]{1,0,2:T(2,128)(2,1)} %copy-done.2, bf16[2,512,1024]{2,0,1:T(2,128)(2,1)} %all_to_all.20), kind=kOutput, calls=%fused_computation.18 | convolution fusion | flops 4194304 | bytes 4194320 | tf_op jit(solution)/shard_map/zrc,ycr->zy/dot_general | solution.py:46
  261.7 0.7 fusion.25
  264.9 0.1 maximum_bitcast_fusion
  265.0 2.9 %psum.7 = f32[1,2]{1,0:T(1,128)} all-reduce(f32[1,2]{1,0:T(1,128)S(1)} %maximum_bitcast_fusion), channel_id=1, replica_groups=mesh['cfg'=1,'pair'=16,'blk'=2] {'blk'}, use_global_device_ids=true, to_apply=%region_0.0 | all-reduce | flops 2 | bytes 16 | tf_op jit(solution)/shard_map/psum | solution.py:48
Async XLA Ops:
  6.5 2.4 copy-start
  6.5 95.1 %all-gather.3.cloned.1.call-start = ((), (), s32[]{:S(2)}) async-start(), calls=%async_computation.2 | async-start | bytes 6291456 | tf_op jit(solution)/shard_map/all_gather | solution.py:25
  8.9 19.1 %copy-start.6 = (s32[16,24,4,4]{1,3,2,0:T(4,128)S(1)}, s32[16,24,4,4]{1,3,2,0:T(4,128)}, u32[]{:S(2)}) copy-start(s32[16,24,4,4]{1,3,2,0:T(4,128)} %param.10) | copy-start | bytes 73732
  89.6 1.6 copy-start.3
  92.6 16.7 %copy-start.4 = (bf16[1,1,1024,512]{3,2,1,0:T(8,128)(2,1)S(1)}, bf16[1,1,1024,512]{3,2,1,0:T(8,128)(2,1)}, u32[]{:S(2)}) copy-start(bf16[1,1,1024,512]{3,2,1,0:T(8,128)(2,1)} %get-tuple-element.5) | copy-start | bytes 3145732
  109.4 3.0 %copy-start.1 = (bf16[32,4,4,2,8,256]{5,4,2,3,1,0:T(8,128)(2,1)S(1)}, bf16[32,4,4,2,8,256]{5,4,2,3,1,0:T(8,128)(2,1)}, u32[]{:S(2)}) copy-start(bf16[32,4,4,2,8,256]{5,4,2,3,1,0:T(8,128)(2,1)} %reshape.43) | copy-start | bytes 12582916
  109.4 3.1 %copy-start.5 = (bf16[1,1,1024,512]{3,2,1,0:T(8,128)(2,1)S(1)}, bf16[1,1,1024,512]{3,2,1,0:T(8,128)(2,1)}, u32[]{:S(2)}) copy-start(bf16[1,1,1024,512]{3,2,1,0:T(8,128)(2,1)} %get-tuple-element.6) | copy-start | bytes 3145732
  138.9 2.7 copy-start.2
  138.9 93.9 %collective-permute-start = (bf16[2,1024,512]{1,0,2:T(2,128)(2,1)S(1)}, bf16[2,1024,512]{1,0,2:T(2,128)(2,1)}, u32[]{:S(2)}, u32[]{:S(2)}) collective-permute-start(bf16[2,1024,512]{1,0,2:T(2,128)(2,1)S(1)} %pad_maximum_fusion), channel_id=1, source_target_pairs={{0,16},{2,18},{4,20},{6,22},{8,24},{10,26},{12,28},{14,30},{16,0},... | collective-permute-start | bytes 6291464 | tf_op jit(solution)/shard_map/ppermute | solution.py:11
Sparse Core Ops, SparseCore 0:
  89.7 11.9 all-gather.2
where the time goes:
time: 276 us; the launch traced here: 275 us
  waiting for transfers between devices  100 us (36%)
  blocking collectives  65.4 us (24%)
  local copies, waits for them, and re-layouts  57.7 us (21%)
  matrix products  24.4 us (9%)
  between operations  16 us (6%)
  other arithmetic  8.21 us (3%)
    ppermute x1, waiting for transfers between devices, partner(): lax.ppermute(value, axis, [(i, i ^ 1 << apart) for i in range(lax.axis_si...  91.1 us
    all_to_all x1, blocking collectives, shards(): lax.all_to_all(combined, 'pair', split_axis=0, concat_axis=0, tiled=True)  57.1 us
    gather x1, local copies, waits for them, and re-layouts, shards(): picked = elementals[pairs[:, 0][:, None], elem_index]  19.1 us
    another operation x2, local copies, waits for them, and re-layouts, shards(): jnp.stack([dressed_real, dressed_imag]).astype(jnp.bfloat16)  10.7 us
    dot_general x1, matrix products, shards(): jnp.einsum('zrc,ycr->zy', dressed, mirror_rows, preferred_element_type=jn...  9.3 us
    all_gather x1, waiting for transfers between devices, shards(): gathered = lax.all_gather(blocks[:, None], 'blk', axis=1, tiled=True)  9.04 us
    ppermute x1, local copies, waits for them, and re-layouts, partner(): lax.ppermute(value, axis, [(i, i ^ 1 << apart) for i in range(lax.axis_si...  8.31 us
    reshape x1, local copies, waits for them, and re-layouts, shards(): shaped = gathered.reshape(2 * peers, NS, NS, 2, entries // NV, NV)  7.7 us
  transfers between devices with their start and end apart: 2, of which 2 were waited for; matrix products, arithmetic and copies ran while one was open for 1% of the time, Pallas kernels for 0%

commit v1 on v0

v1 whole, which is shorter than its diff:
```python
import functools

import jax
import jax.numpy as jnp
from jax import lax
from jax.experimental import pallas as pl
from jax.experimental.pallas import tpu as pltpu
from jax.sharding import PartitionSpec as P

NV = 256
NS = 4
SUB = 16
MESH = pl.DeviceIdType.MESH


def dot(x, y):
    return jnp.dot(x, y, preferred_element_type=jnp.float32)


def kernel(
    peers,
    picked_ref,
    fold_ref,
    prop_ref,
    out_ref,
    ebuf,
    obuf,
    pbuf,
    dbuf,
    rbuf,
    tot,
    psem,
    lsem,
    esend,
    erecv,
    fsend,
    frecv,
    dsend,
    drecv,
    ssend,
    srecv,
):
    me = lax.axis_index("pair")
    core = lax.axis_index("blk")
    other = 1 - core
    hp = peers // 2
    half = me // hp
    place = me % hp
    mirror = (me + hp) % peers
    chunk = picked_ref.shape[1]
    depth = fold_ref.shape[1]
    groups = peers * 2 * chunk // depth
    hg = groups // 2
    hrows = NV // 2

    prop_copy = pltpu.make_async_copy(prop_ref, pbuf, psem)
    prop_copy.start()

    def slot(s, c):
        return ebuf.at[pl.ds(pl.multiple_of((s * 2 + c) * chunk, SUB), chunk)]

    own_copy = pltpu.make_async_copy(picked_ref.at[me], slot(me, core), lsem)
    own_copy.start()

    barrier = pltpu.get_barrier_semaphore()

    def greet(k, _):
        pl.semaphore_signal(
            barrier,
            inc=1,
            device_id={"pair": (me + k) % peers, "blk": core},
            device_id_type=MESH,
        )
        return 0

    lax.fori_loop(1, peers, greet, 0)
    for target in (me, mirror):
        pl.semaphore_signal(
            barrier, inc=1, device_id={"pair": target, "blk": other}, device_id_type=MESH
        )
    pl.semaphore_wait(barrier, peers + 1)

    def send_copy(target):
        return pltpu.make_async_remote_copy(
            src_ref=picked_ref.at[target],
            dst_ref=slot(me, core),
            send_sem=esend.at[target],
            recv_sem=erecv.at[me],
            device_id={"pair": target, "blk": core},
            device_id_type=MESH,
        )

    def arrived(source):
        return pltpu.make_async_remote_copy(
            src_ref=slot(source, core),
            dst_ref=slot(source, core),
            send_sem=esend.at[source],
            recv_sem=erecv.at[source],
            device_id={"pair": me, "blk": other},
            device_id_type=MESH,
        )

    def forward(source, src=None):
        return pltpu.make_async_remote_copy(
            src_ref=slot(source, core) if src is None else src,
            dst_ref=slot(source, core),
            send_sem=fsend.at[source],
            recv_sem=frecv.at[source],
            device_id={"pair": me, "blk": other},
            device_id_type=MESH,
        )

    def handed(source):
        return pltpu.make_async_remote_copy(
            src_ref=slot(source, other),
            dst_ref=slot(source, other),
            send_sem=fsend.at[source],
            recv_sem=frecv.at[source],
            device_id={"pair": me, "blk": other},
            device_id_type=MESH,
        )

    forward(me, picked_ref.at[me]).start()
    send_copy((1 - half) * hp + place).start()

    def send(k, _):
        step = (place + k) % hp
        send_copy((1 - half) * hp + step).start()
        send_copy(half * hp + step).start()
        return 0

    lax.fori_loop(1, hp, send, 0)
    own_copy.wait()

    def block_copy(h, a):
        x = (a + half) % 2
        place_there = 2 * core + x
        return pltpu.make_async_remote_copy(
            src_ref=dbuf.at[:, a, x, pl.ds(pl.multiple_of(h * hrows, hrows), hrows)],
            dst_ref=rbuf.at[:, place_there, pl.ds(pl.multiple_of(h * hrows, hrows), hrows)],
            send_sem=dsend.at[h * NS + a],
            recv_sem=drecv.at[h * NS + place_there],
            device_id={"pair": mirror, "blk": a // 2},
            device_id_type=MESH,
        )

    def block_arrived(h, a):
        rows = pl.ds(pl.multiple_of(h * hrows, hrows), hrows)
        return pltpu.make_async_remote_copy(
            src_ref=rbuf.at[:, a, rows],
            dst_ref=rbuf.at[:, a, rows],
            send_sem=dsend.at[h * NS + a],
            recv_sem=drecv.at[h * NS + a],
            device_id={"pair": mirror, "blk": other},
            device_id_type=MESH,
        )

    for phase in range(2):
        h = half if phase == 0 else 1 - half

        def take(k, _):
            source = h * hp + (place - k + hp) % hp
            arrived(source).wait_recv()
            forward(source).start()
            return 0

        lax.fori_loop(1 - phase, hp, take, 0)

        def pass_on(k, _):
            handed(h * hp + k).wait_recv()
            return 0

        lax.fori_loop(0, hp, pass_on, 0)

        def build(k, _):
            group = h * hg + k
            entries = ebuf[pl.ds(pl.multiple_of(group * depth, SUB), depth), :]
            blocks = dot(fold_ref[...], entries).astype(jnp.bfloat16)
            rows = pl.ds(pl.multiple_of(group * SUB, SUB), SUB)
            for c in range(2):
                for a in range(NS):
                    for b in range(NS):
                        first = ((c * NS + a) * NS + b) * SUB
                        obuf[c, a, rows, b * NV : (b + 1) * NV] = blocks[first : first + SUB]
            return 0

        lax.fori_loop(0, hg, build, 0)
        if phase == 0:
            prop_copy.wait()
        rows = pl.ds(pl.multiple_of(h * hrows, hrows), hrows)

        def dress(j, _):
            x = (j + half) % 2
            columns = pl.ds(pl.multiple_of(x * NV, NV), NV)
            oreal = obuf[0, :, rows, :].reshape(NS * hrows, NS * NV)
            oimag = obuf[1, :, rows, :].reshape(NS * hrows, NS * NV)
            preal = pbuf[0, :, columns]
            pimag = pbuf[1, :, columns]
            dreal = dot(oreal, preal) - dot(oimag, pimag)
            dbuf[0, :, x, rows, :] = dreal.astype(jnp.bfloat16).reshape(NS, hrows, NV)
            dimag = dot(oreal, pimag) + dot(oimag, preal)
            dbuf[1, :, x, rows, :] = dimag.astype(jnp.bfloat16).reshape(NS, hrows, NV)
            block_copy(h, j).start()
            block_copy(h, j + 2).start()
            return 0

        lax.fori_loop(0, 2, dress, 0)

    row = lax.broadcasted_iota(jnp.int32, (hrows, NV), 0)
    column = lax.broadcasted_iota(jnp.int32, (hrows, NV), 1)
    total_real = jnp.zeros((hrows, NV), jnp.float32)
    total_imag = jnp.zeros((hrows, NV), jnp.float32)
    for phase in range(2):
        h = 1 - half if phase == 0 else half
        rows = pl.ds(pl.multiple_of(h * hrows, hrows), hrows)

        def close(a, carry):
            sum_real, sum_imag = carry
            block_arrived(h, a).wait_recv()
            x = (a + half + 1) % 2
            rreal, rimag = rbuf[0, a, rows, :], rbuf[1, a, rows, :]
            dreal, dimag = dbuf[0, a, x], dbuf[1, a, x]
            sum_real += dot(rreal, dreal) - dot(rimag, dimag)
            sum_imag += dot(rreal, dimag) + dot(rimag, dreal)
            return sum_real, sum_imag

        zero = jnp.zeros((hrows, NV), jnp.float32)
        sum_real, sum_imag = lax.fori_loop(0, NS, close, (zero, zero))
        diagonal = row + h * hrows == column
        total_real += jnp.where(diagonal, sum_real, 0.0)
        total_imag += jnp.where(diagonal, sum_imag, 0.0)
    real = jnp.sum(total_real)
    imag = jnp.sum(total_imag)
    lane = lax.broadcasted_iota(jnp.int32, (8, 128), 1)
    mine = half * 2 + core
    tot[mine] = jnp.where(lane == 0, real, jnp.where(lane == 1, imag, 0.0))

    def share(n, pair, blk):
        return pltpu.make_async_remote_copy(
            src_ref=tot.at[mine],
            dst_ref=tot.at[mine],
            send_sem=ssend.at[n],
            recv_sem=srecv.at[mine],
            device_id={"pair": pair, "blk": blk},
            device_id_type=MESH,
        )

    def shared(source):
        return pltpu.make_async_remote_copy(
            src_ref=tot.at[source],
            dst_ref=tot.at[source],
            send_sem=ssend.at[0],
            recv_sem=srecv.at[source],
            device_id={"pair": me, "blk": other},
            device_id_type=MESH,
        )

    shares = [share(0, me, other), share(1, mirror, core), share(2, mirror, other)]
    for copy in shares:
        copy.start()

    def sent(k, _):
        send_copy((me + k) % peers).wait_send()
        return 0

    lax.fori_loop(1, peers, sent, 0)

    def forwarded(k, _):
        forward(k).wait_send()
        return 0

    lax.fori_loop(0, peers, forwarded, 0)
    for h in range(2):
        for a in range(NS):
            block_copy(h, a).wait_send()
    for copy in shares:
        copy.wait_send()
    for source in (half * 2 + other, (1 - half) * 2 + core, (1 - half) * 2 + other):
        shared(source).wait_recv()
    out_ref[...] = ((tot[0] + tot[1]) + (tot[2] + tot[3]))[0:1, 0:2]


def shards(elementals, perambulator, pairs, elem_index, coef_code, term_count):
    peers = lax.axis_size("pair")
    me = lax.axis_index("pair")
    _, nops, parts, entries = elementals.shape
    lines = entries // NV
    sources = SUB // lines
    nterms = elem_index.shape[1]
    columns = perambulator.shape[-1]
    picked = elementals[pairs[:, 0]].reshape(peers, nops * parts * lines, NV)
    used = (jnp.arange(nterms) < term_count[me]).astype(jnp.float32)
    hot = (elem_index[me][:, None] == jnp.arange(nops)[None, :]).astype(jnp.float32)
    weights = coef_code[me].astype(jnp.float32) * 0.5 * used[:, None, None]
    merged = jnp.sum(hot[:, :, None, None] * weights[:, None], axis=0)
    same_part = jnp.eye(parts, dtype=jnp.float32)
    same_line = jnp.eye(SUB, dtype=jnp.float32).reshape(sources, lines, sources, lines)
    fold = (
        merged.transpose(1, 2, 0)[None, :, :, None, None, None, :, None, None]
        * same_part[:, None, None, None, None, None, None, :, None]
        * same_line[None, None, None, :, :, :, None, None, :]
    )
    depth = sources * nops * parts * lines
    fold = fold.astype(jnp.bfloat16).reshape(parts * NS * NS * SUB, depth)
    half_lines = NV
    return pl.pallas_call(
        functools.partial(kernel, peers),
        out_shape=jax.ShapeDtypeStruct((1, 2), jnp.float32),
        in_specs=[
            pl.BlockSpec(memory_space=pl.ANY),
            pl.BlockSpec(memory_space=pltpu.VMEM),
            pl.BlockSpec(memory_space=pl.ANY),
        ],
        out_specs=pl.BlockSpec(memory_space=pltpu.VMEM),
        scratch_shapes=[
            pltpu.VMEM((peers * 2 * nops * parts * lines, NV), jnp.bfloat16),
            pltpu.VMEM((2, NS, NV, NS * NV), jnp.bfloat16),
            pltpu.VMEM((2, NS * NV, columns), jnp.bfloat16),
            pltpu.VMEM((2, NS, 2, NV, NV), jnp.bfloat16),
            pltpu.VMEM((2, NS, half_lines, NV), jnp.bfloat16),
            pltpu.VMEM((4, 8, 128), jnp.float32),
            pltpu.SemaphoreType.DMA,
            pltpu.SemaphoreType.DMA,
            pltpu.SemaphoreType.DMA((peers,)),
            pltpu.SemaphoreType.DMA((peers,)),
            pltpu.SemaphoreType.DMA((peers,)),
            pltpu.SemaphoreType.DMA((peers,)),
            pltpu.SemaphoreType.DMA((2 * NS,)),
            pltpu.SemaphoreType.DMA((2 * NS,)),
            pltpu.SemaphoreType.DMA((3,)),
            pltpu.SemaphoreType.DMA((4,)),
        ],
        compiler_params=pltpu.CompilerParams(
            collective_id=0, has_side_effects=True, vmem_limit_bytes=48 * 1024 * 1024
        ),
    )(picked, fold, perambulator[0])


def solution(mesh):
    return jax.shard_map(
        shards,
        mesh=mesh,
        in_specs=(
            P("cfg", None, None, ("pair", "blk")),
            P(("cfg", "pair"), None, None, "blk"),
            P(),
            P(),
            P(),
            P(),
        ),
        out_specs=P(("cfg", "pair"), None),
        check_vma=False,
    )
```

time: 276 us -> 101 us (0.37)
  waiting for transfers between devices: 100 us -> 0 us
  Pallas kernels: 0 us -> 78.4 us
  blocking collectives: 65.4 us -> 0 us
  local copies, waits for them, and re-layouts: 57.7 us -> 14.4 us
  matrix products: 24.4 us -> 0 us
  between operations: 16 us -> 0.12 us
    ppermute x1 -> x0, waiting for transfers between devices: 91.1 us -> none  [partner(): lax.ppermute(value, axis, [(i, i ^ 1 << apart) for i in range(lax.axis_si...]
    pallas_call x0 -> x1, Pallas kernels: none -> 78.4 us  [shards(): pl.pallas_call(functools.partial(kernel, peers), out_shape=jax.ShapeDtype...]
    all_to_all x2 -> x0, blocking collectives: 62.5 us -> none  [the longest x1 57.1 us: shards(): lax.all_to_all(combined, 'pair', split_axis=0, concat_axis=0, tiled=True)]
    dot_general x6 -> x0, matrix products: 24.4 us -> none  [the longest x1 9.3 us: shards(): jnp.einsum('zrc,ycr->zy', dressed, mirror_rows, preferred_element_type=jn...]
    gather x1, local copies, waits for them, and re-layouts: 19.1 us -> 2.66 us  [shards(): picked = elementals[pairs[:, 0]].reshape(peers, nops * parts * lines, NV)]
    another operation x2 -> x0, local copies, waits for them, and re-layouts: 10.7 us -> none  [shards(): jnp.stack([dressed_real, dressed_imag]).astype(jnp.bfloat16)]
    all_gather x1 -> x0, waiting for transfers between devices: 9.04 us -> none  [shards(): gathered = lax.all_gather(blocks[:, None], 'blk', axis=1, tiled=True)]
    ppermute x1 -> x0, local copies, waits for them, and re-layouts: 8.31 us -> none  [partner(): lax.ppermute(value, axis, [(i, i ^ 1 << apart) for i in range(lax.axis_si...]
  transfers between devices with their start and end apart: 2 -> 0, of which waited for: 2 -> 0; matrix products, arithmetic and copies ran while one was open for 1% -> 0% of each run, Pallas kernels for 0% -> 0%
where the time goes in v1:
time: 101 us
  Pallas kernels  78.4 us (78%)
  local copies, waits for them, and re-layouts  14.4 us (14%)
  other arithmetic  7.83 us (8%)
    pallas_call x1, Pallas kernels, shards(): pl.pallas_call(functools.partial(kernel, peers), out_shape=jax.ShapeDtype...  78.4 us
    convert_element_type x1, local copies, waits for them, and re-layouts, shards(): fold = fold.astype(jnp.bfloat16).reshape(parts * NS * NS * SUB, depth)  6.89 us
    convert_element_type x1, other arithmetic, shards(): fold = fold.astype(jnp.bfloat16).reshape(parts * NS * NS * SUB, depth)  6.19 us
    gather x1, local copies, waits for them, and re-layouts, shards(): picked = elementals[pairs[:, 0]].reshape(peers, nops * parts * lines, NV)  2.66 us
    unnamed x7, local copies, waits for them, and re-layouts  2.11 us

profile of v1, /device:TPU:0, one launch (start us, length us, event | category | flops | bytes accessed | tf_op | source)
XLA Modules:
  0.0 100.8 jit_solution(15482005778258522766)
XLA Ops:
  0.0 0.0 copy-start
  0.0 1.3 %dynamic_slice.11 = s32[1]{0:T(128)} dynamic-slice(s32[16]{0:T(128)} %param.11, s32[]{:T(128)S(6)} %select_n.10), dynamic_slice_sizes={1} | dynamic-slice | bytes 12 | tf_op jit(solution)/shard_map/dynamic_slice | solution.py:292
  1.3 0.6 compare_select_fusion.1
  2.0 0.7 bitcast_multiply_fusion
  2.7 0.7 dynamic-slice_bitcast_fusion
  3.4 0.1 multiply_reduce_fusion
  3.5 0.1 broadcast_multiply_fusion
  3.6 0.1 compare_convert_fusion
  3.7 0.0 copy-start.2
  3.7 6.2 %multiply_convert_fusion = bf16[2,4,4,2,8,2,8,2,8]{8,7,6,5,4,3,2,1,0:T(2,128)(2,1)} fusion(f32[2,8,2,8]{3,2,1,0:T(2,128)S(1)} %compare_convert_fusion, f32[2,4,4,8,2]{4,3,2,1,0:T(8,128)S(1)} %broadcast_multiply_fusion), kind=kLoop, calls=%fused_computation.1 | loop fusion | flops 262144 | bytes 265216 | tf_op jit(solution)/shard_map/convert_element_type | solution.py:304
  9.9 6.9 %convert_element_type.49.fold_ref = bf16[512,256]{1,0:T(8,128)(2,1)S(1)} reshape(bf16[2,4,4,2,8,2,8,2,8]{8,7,6,5,4,3,2,1,0:T(2,128)(2,1)} %multiply_convert_fusion) | data formatting | bytes 524288 | tf_op jit(solution)/shard_map/convert_element_type | solution.py:304
  16.8 0.0 copy-done.2
  16.8 0.0 copy-done
  16.8 2.7 %gather_fusion = bf16[16,8,2,2048]{3,2,1,0:T(2,128)(2,1)S(1)} fusion(bf16[16,8,2,2048]{3,2,1,0:T(2,128)(2,1)S(1)} %copy-done, s32[1024]{0:T(1024)S(1)} %pad_clamp_fusion), kind=kCustom, calls=%fused_computation | custom fusion | bytes 2097216 | tf_op jit(solution)/shard_map/gather | solution.py:291
  19.5 0.7 reshape.85.picked_ref
  20.2 0.0 copy-start.1
  20.2 1.6 %copy-done.1 = bf16[1,2,1024,512]{3,2,1,0:T(8,128)(2,1)S(1)} copy-done((bf16[1,2,1024,512]{3,2,1,0:T(8,128)(2,1)S(1)}, bf16[1,2,1024,512]{3,2,1,0:T(8,128)(2,1)}, u32[]{:S(2)}) %copy-start.1) | copy-done | bytes 2097176
  21.8 78.4 %shard_map.64 = f32[1,2]{1,0:T(1,128)S(1)} custom-call(bf16[16,128,256]{2,1,0:T(8,128)(2,1)S(1)} %reshape.85.picked_ref, bf16[512,256]{1,0:T(8,128)(2,1)S(1)} %convert_element_type.49.fold_ref, bf16[2,1024,512]{2,1,0:T(8,128)(2,1)S(1)} %bitcast.9), custom_call_target="tpu_custom_call" | custom-call | tf_op jit(solution)/shard_map/pallas_call | solution.py:306
  100.3 0.5 copy.9
  (5 shorter events, 0.0 us)
Async XLA Ops:
  0.0 16.8 %copy-start = (bf16[16,8,2,2048]{3,2,1,0:T(2,128)(2,1)S(1)}, bf16[16,8,2,2048]{3,2,1,0:T(2,128)(2,1)}, u32[]{:S(2)}) copy-start(bf16[16,8,2,2048]{3,2,1,0:T(2,128)(2,1)} %param.6) | copy-start | bytes 3145732
  3.7 13.1 %copy-start.2 = (s32[16,2]{0,1:T(2,128)S(1)}, s32[16,2]{0,1:T(2,128)}, u32[]{:S(2)}) copy-start(s32[16,2]{0,1:T(2,128)} %param.8) | copy-start | bytes 388
  20.2 1.6 %copy-start.1 = (bf16[1,2,1024,512]{3,2,1,0:T(8,128)(2,1)S(1)}, bf16[1,2,1024,512]{3,2,1,0:T(8,128)(2,1)}, u32[]{:S(2)}) copy-start(bf16[1,2,1024,512]{3,2,1,0:T(8,128)(2,1)} %param.7) | copy-start | bytes 6291460

commit v2 on v1

--- a/solution.py
+++ b/solution.py
@@ -19,10 +19,16 @@
 
 def kernel(
     peers,
-    picked_ref,
-    fold_ref,
+    lines,
+    pairs_ref,
+    count_ref,
+    index_ref,
+    code_ref,
+    elem_ref,
     prop_ref,
     out_ref,
+    sbuf,
+    fold_ref,
     ebuf,
     obuf,
     pbuf,
@@ -30,7 +36,6 @@
     rbuf,
     tot,
     psem,
-    lsem,
     esend,
     erecv,
     fsend,
@@ -47,7 +52,7 @@
     half = me // hp
     place = me % hp
     mirror = (me + hp) % peers
-    chunk = picked_ref.shape[1]
+    chunk = elem_ref.shape[1]
     depth = fold_ref.shape[1]
     groups = peers * 2 * chunk // depth
     hg = groups // 2
@@ -58,9 +63,6 @@
 
     def slot(s, c):
         return ebuf.at[pl.ds(pl.multiple_of((s * 2 + c) * chunk, SUB), chunk)]
-
-    own_copy = pltpu.make_async_copy(picked_ref.at[me], slot(me, core), lsem)
-    own_copy.start()
 
     barrier = pltpu.get_barrier_semaphore()
 
@@ -82,7 +84,7 @@
 
     def send_copy(target):
         return pltpu.make_async_remote_copy(
-            src_ref=picked_ref.at[target],
+            src_ref=sbuf.at[target],
             dst_ref=slot(me, core),
             send_sem=esend.at[target],
             recv_sem=erecv.at[me],
@@ -100,9 +102,9 @@
             device_id_type=MESH,
         )
 
-    def forward(source, src=None):
-        return pltpu.make_async_remote_copy(
-            src_ref=slot(source, core) if src is None else src,
+    def forward(source):
+        return pltpu.make_async_remote_copy(
+            src_ref=slot(source, core),
             dst_ref=slot(source, core),
             send_sem=fsend.at[source],
             recv_sem=frecv.at[source],
@@ -120,17 +122,46 @@
             device_id_type=MESH,
         )
 
-    forward(me, picked_ref.at[me]).start()
-    send_copy((1 - half) * hp + place).start()
+    def post(target):
+        sbuf[target] = elem_ref[pairs_ref[target, 0]]
+        send_copy(target).start()
+
+    post((1 - half) * hp + place)
+    own_rows = pl.ds(pl.multiple_of((me * 2 + core) * chunk, SUB), chunk)
+    ebuf[own_rows, :] = elem_ref[pairs_ref[me, 0]]
+    forward(me).start()
 
     def send(k, _):
         step = (place + k) % hp
-        send_copy((1 - half) * hp + step).start()
-        send_copy(half * hp + step).start()
+        post((1 - half) * hp + step)
+        post(half * hp + step)
         return 0
 
     lax.fori_loop(1, hp, send, 0)
-    own_copy.wait()
+
+    nterms = index_ref.shape[1]
+    rows = fold_ref.shape[0]
+    spin = lax.broadcasted_iota(jnp.int32, (rows, NS * NS), 0) // SUB % (NS * NS)
+    pick = (spin == lax.broadcasted_iota(jnp.int32, (rows, NS * NS), 1)).astype(jnp.float32)
+    codes = code_ref[me].astype(jnp.float32).astype(jnp.bfloat16)
+    spread = lax.dot_general(
+        pick.astype(jnp.bfloat16),
+        codes,
+        (((1,), (1,)), ((), ())),
+        preferred_element_type=jnp.float32,
+    ).astype(jnp.bfloat16)
+    entry = lax.broadcasted_iota(jnp.int32, (depth, nterms), 0) % chunk // (2 * lines)
+    term = lax.broadcasted_iota(jnp.int32, (depth, nterms), 1)
+    uses = (entry == index_ref[pl.ds(me, 1), :]) & (term < count_ref[me])
+    halves = jnp.where(uses, 0.5, 0.0).astype(jnp.bfloat16)
+    weights = lax.dot_general(
+        spread, halves, (((1,), (1,)), ((), ())), preferred_element_type=jnp.float32
+    )
+    out_row = lax.broadcasted_iota(jnp.int32, (rows, depth), 0)
+    in_row = lax.broadcasted_iota(jnp.int32, (rows, depth), 1)
+    same_part = out_row // (NS * NS * SUB) == in_row // lines % 2
+    same_line = out_row % SUB == in_row // chunk * lines + in_row % lines
+    fold_ref[...] = jnp.where(same_part & same_line, weights, 0.0).astype(jnp.bfloat16)
 
     def block_copy(h, a):
         x = (a + half) % 2
@@ -282,44 +313,35 @@
 
 def shards(elementals, perambulator, pairs, elem_index, coef_code, term_count):
     peers = lax.axis_size("pair")
-    me = lax.axis_index("pair")
     _, nops, parts, entries = elementals.shape
     lines = entries // NV
     sources = SUB // lines
     nterms = elem_index.shape[1]
     columns = perambulator.shape[-1]
-    picked = elementals[pairs[:, 0]].reshape(peers, nops * parts * lines, NV)
-    used = (jnp.arange(nterms) < term_count[me]).astype(jnp.float32)
-    hot = (elem_index[me][:, None] == jnp.arange(nops)[None, :]).astype(jnp.float32)
-    weights = coef_code[me].astype(jnp.float32) * 0.5 * used[:, None, None]
-    merged = jnp.sum(hot[:, :, None, None] * weights[:, None], axis=0)
-    same_part = jnp.eye(parts, dtype=jnp.float32)
-    same_line = jnp.eye(SUB, dtype=jnp.float32).reshape(sources, lines, sources, lines)
-    fold = (
-        merged.transpose(1, 2, 0)[None, :, :, None, None, None, :, None, None]
-        * same_part[:, None, None, None, None, None, None, :, None]
-        * same_line[None, None, None, :, :, :, None, None, :]
-    )
-    depth = sources * nops * parts * lines
-    fold = fold.astype(jnp.bfloat16).reshape(parts * NS * NS * SUB, depth)
-    half_lines = NV
+    chunk = nops * parts * lines
+    slices = elementals.reshape(elementals.shape[0], chunk, NV)
+    codes = coef_code.reshape(peers, nterms, NS * NS)
     return pl.pallas_call(
-        functools.partial(kernel, peers),
+        functools.partial(kernel, peers, lines),
         out_shape=jax.ShapeDtypeStruct((1, 2), jnp.float32),
         in_specs=[
-            pl.BlockSpec(memory_space=pl.ANY),
+            pl.BlockSpec(memory_space=pltpu.SMEM),
+            pl.BlockSpec(memory_space=pltpu.SMEM),
+            pl.BlockSpec(memory_space=pltpu.VMEM),
+            pl.BlockSpec(memory_space=pltpu.VMEM),
             pl.BlockSpec(memory_space=pltpu.VMEM),
             pl.BlockSpec(memory_space=pl.ANY),
         ],
         out_specs=pl.BlockSpec(memory_space=pltpu.VMEM),
         scratch_shapes=[
-            pltpu.VMEM((peers * 2 * nops * parts * lines, NV), jnp.bfloat16),
+            pltpu.VMEM((peers, chunk, NV), jnp.bfloat16),
+            pltpu.VMEM((parts * NS * NS * SUB, sources * chunk), jnp.bfloat16),
+            pltpu.VMEM((peers * 2 * chunk, NV), jnp.bfloat16),
             pltpu.VMEM((2, NS, NV, NS * NV), jnp.bfloat16),
             pltpu.VMEM((2, NS * NV, columns), jnp.bfloat16),
             pltpu.VMEM((2, NS, 2, NV, NV), jnp.bfloat16),
-            pltpu.VMEM((2, NS, half_lines, NV), jnp.bfloat16),
+            pltpu.VMEM((2, NS, NV, NV), jnp.bfloat16),
             pltpu.VMEM((4, 8, 128), jnp.float32),
-            pltpu.SemaphoreType.DMA,
             pltpu.SemaphoreType.DMA,
             pltpu.SemaphoreType.DMA((peers,)),
             pltpu.SemaphoreType.DMA((peers,)),
@@ -333,7 +355,7 @@
         compiler_params=pltpu.CompilerParams(
             collective_id=0, has_side_effects=True, vmem_limit_bytes=48 * 1024 * 1024
         ),
-    )(picked, fold, perambulator[0])
+    )(pairs, term_count, elem_index, codes, slices, perambulator[0])
 
 
 def solution(mesh):

time: 101 us -> 83.4 us (0.83)
  local copies, waits for them, and re-layouts: 14.4 us -> 4.18 us
  other arithmetic: 7.83 us -> 0 us
    convert_element_type x1 -> x0, local copies, waits for them, and re-layouts: 6.89 us -> none  [shards(): fold = fold.astype(jnp.bfloat16).reshape(parts * NS * NS * SUB, depth)]
    convert_element_type x4 -> x0, other arithmetic: 6.28 us -> none  [the longest x1 6.19 us: shards(): fold = fold.astype(jnp.bfloat16).reshape(parts * NS * NS * SUB, depth)]
    gather x1 -> x0, local copies, waits for them, and re-layouts: 2.66 us -> none  [shards(): picked = elementals[pairs[:, 0]].reshape(peers, nops * parts * lines, NV)]
    reshape x1 -> x2, local copies, waits for them, and re-layouts: 0.71 us -> 2.75 us  [the longest x1 1.74 us: shards(): slices = elementals.reshape(elementals.shape[0], chunk, NV)]
    mul x3 -> x0, other arithmetic: 1.43 us -> none  [the longest x2 1.35 us: shards(): weights = coef_code[me].astype(jnp.float32) * 0.5 * used[:, None, None]]
    dynamic_slice x1 -> x0, local copies, waits for them, and re-layouts: 1.33 us -> none  [shards(): used = (jnp.arange(nterms) < term_count[me]).astype(jnp.float32)]
    unnamed x7 -> x8, local copies, waits for them, and re-layouts: 2.11 us -> 1.43 us
where the time goes in v2:
time: 83.4 us; the launch traced here: 83.3 us
  Pallas kernels  79 us (95%)
  local copies, waits for them, and re-layouts  4.18 us (5%)
    pallas_call x1, Pallas kernels, shards(): pl.pallas_call(functools.partial(kernel, peers, lines), out_shape=jax.Sha...  79 us
    reshape x1, local copies, waits for them, and re-layouts, shards(): slices = elementals.reshape(elementals.shape[0], chunk, NV)  1.74 us

profile of v2, /device:TPU:0, one launch (start us, length us, event | category | flops | bytes accessed | tf_op | source)
XLA Modules:
  0.0 83.3 jit_solution(8295647971693445552)
XLA Ops:
  0.0 0.0 copy-start.2
  0.0 0.0 copy-start.1
  0.0 0.0 copy-start
  0.0 0.9 %copy.10.pairs_ref = s32[16,2]{1,0:T(8,128)S(1)} copy(s32[16,2]{0,1:T(2,128)} %param.8) | data formatting | bytes 256 | tf_op args[2]
  0.9 1.0 %copy.11.code_ref = s32[16,24,16]{2,1,0:T(8,128)S(1)} copy(s32[16,24,16]{1,2,0:T(8,128)} %bitcast.3) | data formatting | bytes 49152 | tf_op jit(solution)/shard_map/reshape | solution.py:323
  1.9 1.7 %reshape.7.elem_ref = bf16[16,128,256]{2,1,0:T(8,128)(2,1)S(1)} reshape(bf16[16,8,2,2048]{3,2,1,0:T(2,128)(2,1)} %param.6) | data formatting | bytes 2097152 | tf_op jit(solution)/shard_map/reshape | solution.py:322
  3.7 0.0 copy-done.2
  3.7 0.0 copy-done.1
  3.7 0.0 copy-done
  3.7 79.0 %shard_map.64 = f32[1,2]{1,0:T(1,128)S(1)} custom-call(s32[16,2]{1,0:T(8,128)S(1)} %copy.10.pairs_ref, s32[16]{0:T(128)S(1)} %copy-done.2, s32[16,24]{1,0:T(8,128)S(1)} %copy-done.1, s32[16,24,16]{2,1,0:T(8,128)S(1)} %copy.11.code_ref, bf16[16,128,256]{2,1,0:T(8,128)(2,1)S(1)} %reshape.7.elem_ref, bf16[2,1024,512]{2,1,0:T(8,128)(2,1)S(1)} %bitcast.2), custom_call_target="tpu_custom_call" | custom-call | tf_op jit(solution)/shard_map/pallas_call | solution.py:324
  82.8 0.5 copy.15
Async XLA Ops:
  0.0 3.7 %copy-start.2 = (s32[16]{0:T(128)S(1)}, s32[16]{0:T(128)}, u32[]{:S(2)}) copy-start(s32[16]{0:T(128)} %count_ref.1) | copy-start | bytes 196
  0.0 3.7 %copy-start.1 = (s32[16,24]{1,0:T(8,128)S(1)}, s32[16,24]{1,0:T(8,128)}, u32[]{:S(2)}) copy-start(s32[16,24]{1,0:T(8,128)} %index_ref.1) | copy-start | bytes 4612
  0.0 3.7 %copy-start = (bf16[1,2,1024,512]{3,2,1,0:T(8,128)(2,1)S(1)}, bf16[1,2,1024,512]{3,2,1,0:T(8,128)(2,1)}, u32[]{:S(2)}) copy-start(bf16[1,2,1024,512]{3,2,1,0:T(8,128)(2,1)} %param.7) | copy-start | bytes 6291460

commit v3 on v2

--- a/solution.py
+++ b/solution.py
@@ -80,6 +80,14 @@
         pl.semaphore_signal(
             barrier, inc=1, device_id={"pair": target, "blk": other}, device_id_type=MESH
         )
+
+    def fill(k, _):
+        sbuf[k] = elem_ref[pairs_ref[k, 0]]
+        return 0
+
+    lax.fori_loop(0, peers, fill, 0)
+    own_rows = pl.ds(pl.multiple_of((me * 2 + core) * chunk, SUB), chunk)
+    ebuf[own_rows, :] = elem_ref[pairs_ref[me, 0]]
     pl.semaphore_wait(barrier, peers + 1)
 
     def send_copy(target):
@@ -122,22 +130,28 @@
             device_id_type=MESH,
         )
 
-    def post(target):
-        sbuf[target] = elem_ref[pairs_ref[target, 0]]
-        send_copy(target).start()
-
-    post((1 - half) * hp + place)
-    own_rows = pl.ds(pl.multiple_of((me * 2 + core) * chunk, SUB), chunk)
-    ebuf[own_rows, :] = elem_ref[pairs_ref[me, 0]]
+    def near(k):
+        send_copy(half * hp + (place + k) % hp).start()
+
+    def far(k):
+        send_copy((1 - half) * hp + (place + k) % hp).start()
+
+    def send_mixed(k, _):
+        far(k)
+        near(2 * k + 1)
+        near(2 * k + 2)
+        return 0
+
+    def send_far(k, _):
+        far(k)
+        return 0
+
+    mixed = (hp - 1) // 2
+    lax.fori_loop(0, mixed, send_mixed, 0)
     forward(me).start()
-
-    def send(k, _):
-        step = (place + k) % hp
-        post((1 - half) * hp + step)
-        post(half * hp + step)
-        return 0
-
-    lax.fori_loop(1, hp, send, 0)
+    far(mixed)
+    near(hp - 1)
+    lax.fori_loop(mixed + 1, hp, send_far, 0)
 
     nterms = index_ref.shape[1]
     rows = fold_ref.shape[0]

time: 83.4 us -> 83.4 us (level)
  no operation moved by 1% of the time
where the time goes in v3:
time: 83.4 us; the launch traced here: 83.3 us
  Pallas kernels  79 us (95%)
  local copies, waits for them, and re-layouts  4.18 us (5%)
    pallas_call x1, Pallas kernels, shards(): pl.pallas_call(functools.partial(kernel, peers, lines), out_shape=jax.Sha...  79 us
    reshape x1, local copies, waits for them, and re-layouts, shards(): slices = elementals.reshape(elementals.shape[0], chunk, NV)  1.74 us

profile of v3, /device:TPU:0, one launch (start us, length us, event | category | flops | bytes accessed | tf_op | source)
XLA Modules:
  0.0 83.3 jit_solution(14061428720654455422)
XLA Ops:
  0.0 0.0 copy-start.2
  0.0 0.0 copy-start.1
  0.0 0.0 copy-start
  0.0 0.9 %copy.10.pairs_ref = s32[16,2]{1,0:T(8,128)S(1)} copy(s32[16,2]{0,1:T(2,128)} %param.8) | data formatting | bytes 256 | tf_op args[2]
  0.9 1.0 %copy.11.code_ref = s32[16,24,16]{2,1,0:T(8,128)S(1)} copy(s32[16,24,16]{1,2,0:T(8,128)} %bitcast.3) | data formatting | bytes 49152 | tf_op jit(solution)/shard_map/reshape | solution.py:337
  1.9 1.7 %reshape.7.elem_ref = bf16[16,128,256]{2,1,0:T(8,128)(2,1)S(1)} reshape(bf16[16,8,2,2048]{3,2,1,0:T(2,128)(2,1)} %param.6) | data formatting | bytes 2097152 | tf_op jit(solution)/shard_map/reshape | solution.py:336
  3.7 0.0 copy-done.2
  3.7 0.0 copy-done.1
  3.7 0.0 copy-done
  3.7 79.0 %shard_map.64 = f32[1,2]{1,0:T(1,128)S(1)} custom-call(s32[16,2]{1,0:T(8,128)S(1)} %copy.10.pairs_ref, s32[16]{0:T(128)S(1)} %copy-done.2, s32[16,24]{1,0:T(8,128)S(1)} %copy-done.1, s32[16,24,16]{2,1,0:T(8,128)S(1)} %copy.11.code_ref, bf16[16,128,256]{2,1,0:T(8,128)(2,1)S(1)} %reshape.7.elem_ref, bf16[2,1024,512]{2,1,0:T(8,128)(2,1)S(1)} %bitcast.2), custom_call_target="tpu_custom_call" | custom-call | tf_op jit(solution)/shard_map/pallas_call | solution.py:338
  82.7 0.5 copy.15
Async XLA Ops:
  0.0 3.7 %copy-start.2 = (s32[16]{0:T(128)S(1)}, s32[16]{0:T(128)}, u32[]{:S(2)}) copy-start(s32[16]{0:T(128)} %count_ref.1) | copy-start | bytes 196
  0.0 3.7 %copy-start.1 = (s32[16,24]{1,0:T(8,128)S(1)}, s32[16,24]{1,0:T(8,128)}, u32[]{:S(2)}) copy-start(s32[16,24]{1,0:T(8,128)} %index_ref.1) | copy-start | bytes 4612
  0.0 3.7 %copy-start = (bf16[1,2,1024,512]{3,2,1,0:T(8,128)(2,1)S(1)}, bf16[1,2,1024,512]{3,2,1,0:T(8,128)(2,1)}, u32[]{:S(2)}) copy-start(bf16[1,2,1024,512]{3,2,1,0:T(8,128)(2,1)} %param.7) | copy-start | bytes 6291460
